TPU v7x, 512 devices: a whole 4x4x16 slice. The times are simulated.
512 devices in a mesh: ctx: 64 (over x_lo, z, core), tp: 8 (over x_hi, y).
Axes of the slice: x: 4 (x_hi: 2, x_lo: 2; x = x_hi * 2 + x_lo), y: 4, z: 16, core: 2. Of those that a mesh axis runs over, the one named last changes fastest.
Arguments:
- query: bfloat16 [8192, 4096], P('ctx', 'tp'), as said below
- key_proj: bfloat16 [8192, 4096], P('ctx', 'tp'), may hold values from -6 to 6
- value_proj: bfloat16 [8192, 4096], P('ctx', 'tp'), may hold values from -6 to 6
- filter_taps: bfloat16 [8192, 4096], P('ctx', 'tp'), may hold values from -6 to 6
- grad_out: bfloat16 [8192, 4096], P('ctx', 'tp'), may hold values from -6 to 6
Outputs:
- mixer_out: bfloat16 [8192, 4096], P('ctx', 'tp')
- dquery: bfloat16 [8192, 4096], P('ctx', 'tp')
- dkey: bfloat16 [8192, 4096], P('ctx', 'tp')
- dvalue: bfloat16 [8192, 4096], P('ctx', 'tp')
- dtaps: bfloat16 [8192, 4096], P('ctx', 'tp')
Inputs may be any that keep to these rules, and one draw needn't show every extreme that they name: Entries of query are real values of either sign.
All inputs are finite; a program needn't handle non-finite values.
Results may differ from a plain program's by a relative error of at most 0.0085.
Values may be sent and summed in bfloat16 or wider, within the bound.
A program may use at most 64 MiB of HBM per device.

v0:
```python
import math
import jax
import jax.numpy as jnp
from jax import lax
from jax.sharding import PartitionSpec as P

precise = lax.Precision.HIGHEST


def dft_tables(size_count):
    index = jnp.arange(size_count, dtype=jnp.int32)
    angle = (
        2.0
        * math.pi
        / size_count
        * (index[:, None] * index[None, :] % size_count).astype(jnp.float32)
    )
    return (jnp.cos(angle), jnp.sin(angle))


def twiddles(row_count, col_count):
    total = row_count * col_count
    row_index = jnp.arange(row_count, dtype=jnp.int32)
    col_index = jnp.arange(col_count, dtype=jnp.int32)
    angle = (
        2.0
        * math.pi
        / total
        * (row_index[:, None] * col_index[None, :] % total).astype(jnp.float32)
    )
    return (jnp.cos(angle), jnp.sin(angle))


def left_apply(table, blocks):
    return jnp.einsum("ka,cab->ckb", table, blocks, precision=precise)


def right_apply(blocks, table):
    return jnp.einsum("cka,ab->ckb", blocks, table, precision=precise)


def spectrum(signal):
    channels, length = signal.shape
    total = 2 * length
    row_count = 128
    col_count = total // row_count
    padded = jnp.concatenate(
        [signal.astype(jnp.float32), jnp.zeros((channels, length), jnp.float32)], axis=1
    )
    padded = padded.reshape(channels, row_count, col_count)
    cos_rows, sin_rows = dft_tables(row_count)
    cos_cols, sin_cols = dft_tables(col_count)
    cos_twist, sin_twist = twiddles(row_count, col_count)
    first_real = left_apply(cos_rows, padded)
    first_imag = -left_apply(sin_rows, padded)
    turned_real = first_real * cos_twist + first_imag * sin_twist
    turned_imag = first_imag * cos_twist - first_real * sin_twist
    spec_real = right_apply(turned_real, cos_cols) + right_apply(turned_imag, sin_cols)
    spec_imag = right_apply(turned_imag, cos_cols) - right_apply(turned_real, sin_cols)
    return (spec_real, spec_imag)


def signal_of(spec_real, spec_imag, length):
    channels, row_count, col_count = spec_real.shape
    total = row_count * col_count
    cos_rows, sin_rows = dft_tables(row_count)
    cos_cols, sin_cols = dft_tables(col_count)
    cos_twist, sin_twist = twiddles(row_count, col_count)
    back_real = right_apply(spec_real, cos_cols) - right_apply(spec_imag, sin_cols)
    back_imag = right_apply(spec_imag, cos_cols) + right_apply(spec_real, sin_cols)
    turned_real = back_real * cos_twist - back_imag * sin_twist
    turned_imag = back_imag * cos_twist + back_real * sin_twist
    values = left_apply(cos_rows, turned_real) - left_apply(sin_rows, turned_imag)
    return values.reshape(channels, total)[:, :length] / total


def times_plain(left_real, left_imag, right_real, right_imag):
    return (
        left_real * right_real - left_imag * right_imag,
        left_real * right_imag + left_imag * right_real,
    )


def times_conj(left_real, left_imag, right_real, right_imag):
    return (
        left_real * right_real + left_imag * right_imag,
        left_imag * right_real - left_real * right_imag,
    )


def channel_total(values):
    return lax.psum(values, "tp")


def per_device(query, key_proj, value_proj, filter_taps, grad_out):
    length = query.shape[0] * lax.axis_size("ctx")
    width = query.shape[1] * lax.axis_size("tp")
    filter_scale = 1.0 / math.sqrt(length)
    key_cols, value_cols, taps_cols = (
        lax.all_to_all(key_proj.T, "ctx", split_axis=0, concat_axis=1, tiled=True),
        lax.all_to_all(value_proj.T, "ctx", split_axis=0, concat_axis=1, tiled=True),
        lax.all_to_all(filter_taps.T, "ctx", split_axis=0, concat_axis=1, tiled=True),
    )
    mixed_cols = (key_cols.astype(jnp.float32) * value_cols.astype(jnp.float32)).astype(
        jnp.bfloat16
    )
    taps_real, taps_imag = spectrum(taps_cols)
    mixed_real, mixed_imag = spectrum(mixed_cols)
    conv_real, conv_imag = times_plain(mixed_real, mixed_imag, taps_real, taps_imag)
    conv_cols = (filter_scale * signal_of(conv_real, conv_imag, length)).astype(jnp.bfloat16)
    conv_rows = lax.all_to_all(conv_cols, "ctx", split_axis=1, concat_axis=0, tiled=True).T
    conv_float = conv_rows.astype(jnp.float32)
    query_float = query.astype(jnp.float32)
    gated = query_float * conv_float
    upstream = grad_out.astype(jnp.float32)
    square_sum = channel_total(jnp.sum(gated * gated, axis=1))
    inverse_rms = lax.rsqrt(square_sum / width + 1e-05)
    mixer_out = (gated * inverse_rms[:, None]).astype(jnp.bfloat16)
    dots = channel_total(jnp.sum(upstream * gated, axis=1)) / width
    dgated = inverse_rms[:, None] * upstream - (inverse_rms**3 * dots)[:, None] * gated
    dquery = (dgated * conv_float).astype(jnp.bfloat16)
    gconv = (dgated * query_float).astype(jnp.bfloat16)
    grad_cols = lax.all_to_all(gconv.T, "ctx", split_axis=0, concat_axis=1, tiled=True)
    grad_real, grad_imag = spectrum(grad_cols)
    back_real, back_imag = times_conj(grad_real, grad_imag, taps_real, taps_imag)
    dmixed_cols = (filter_scale * signal_of(back_real, back_imag, length)).astype(jnp.bfloat16)
    tap_real, tap_imag = times_conj(grad_real, grad_imag, mixed_real, mixed_imag)
    dtaps_cols = (filter_scale * signal_of(tap_real, tap_imag, length)).astype(jnp.bfloat16)
    dmixed_float = dmixed_cols.astype(jnp.float32)
    dkey_cols = (dmixed_float * value_cols.astype(jnp.float32)).astype(jnp.bfloat16)
    dvalue_cols = (dmixed_float * key_cols.astype(jnp.float32)).astype(jnp.bfloat16)
    dkey_back, dvalue_back, dtaps_back = (
        lax.all_to_all(dkey_cols, "ctx", split_axis=1, concat_axis=0, tiled=True),
        lax.all_to_all(dvalue_cols, "ctx", split_axis=1, concat_axis=0, tiled=True),
        lax.all_to_all(dtaps_cols, "ctx", split_axis=1, concat_axis=0, tiled=True),
    )
    dkey = dkey_back.T
    dvalue = dvalue_back.T
    dtaps = dtaps_back.T
    return (mixer_out, dquery, dkey, dvalue, dtaps)


def solution(mesh):
    in_specs = (P("ctx", "tp"), P("ctx", "tp"), P("ctx", "tp"), P("ctx", "tp"), P("ctx", "tp"))
    out_specs = (P("ctx", "tp"), P("ctx", "tp"), P("ctx", "tp"), P("ctx", "tp"), P("ctx", "tp"))
    return jax.shard_map(
        per_device, mesh=mesh, in_specs=in_specs, out_specs=out_specs, check_vma=False
    )
```

profile of v0, /device:TPU:1, one launch (start us, length us, event | category | flops | bytes accessed | tf_op | source)
XLA Modules:
  0.0 244.5 jit_solution(10890862937073430349)
XLA Ops:
  0.6 1.7 copy.86
  2.3 18.2 %all-to-all-start = ((bf16[64,8,128]{2,1,0:T(8,128)(2,1)}), bf16[64,8,128]{2,1,0:T(8,128)(2,1)S(1)}, u32[]{:S(2)}, u32[]{:S(2)}) async-start(bf16[64,8,128]{2,1,0:T(8,128)(2,1)} %bitcast.1), calls=%async_computation | async-start | bytes 262144 | tf_op jit(solution)/shard_map/all_to_all | solution.py:100
  21.3 16.4 %all-to-all-done = bf16[64,8,128]{2,1,0:T(8,128)(2,1)S(1)} async-done(((bf16[64,8,128]{2,1,0:T(8,128)(2,1)}), bf16[64,8,128]{2,1,0:T(8,128)(2,1)S(1)}, u32[]{:S(2)}, u32[]{:S(2)}) %all-to-all-start) | async-done | bytes 131104 | tf_op jit(solution)/shard_map/all_to_all | solution.py:100
  37.6 4.4 %all-to-all-start.2 = ((bf16[64,8,128]{2,1,0:T(8,128)(2,1)}), bf16[64,8,128]{2,1,0:T(8,128)(2,1)S(1)}, u32[]{:S(2)}, u32[]{:S(2)}) async-start(bf16[64,8,128]{2,1,0:T(8,128)(2,1)} %bitcast.13), calls=%async_computation.2 | async-start | bytes 262144 | tf_op jit(solution)/shard_map/all_to_all | solution.py:102
  44.1 15.2 %all-to-all-done.2 = bf16[64,8,128]{2,1,0:T(8,128)(2,1)S(1)} async-done(((bf16[64,8,128]{2,1,0:T(8,128)(2,1)}), bf16[64,8,128]{2,1,0:T(8,128)(2,1)S(1)}, u32[]{:S(2)}, u32[]{:S(2)}) %all-to-all-start.2) | async-done | bytes 131104 | tf_op jit(solution)/shard_map/all_to_all | solution.py:102
  59.3 4.6 %all-to-all-start.1 = ((bf16[64,8,128]{2,1,0:T(8,128)(2,1)}), bf16[64,8,128]{2,1,0:T(8,128)(2,1)S(1)}, u32[]{:S(2)}, u32[]{:S(2)}) async-start(bf16[64,8,128]{2,1,0:T(8,128)(2,1)} %bitcast.5), calls=%async_computation.1 | async-start | bytes 262144 | tf_op jit(solution)/shard_map/all_to_all | solution.py:101
  65.3 15.7 %all-to-all-done.1 = bf16[64,8,128]{2,1,0:T(8,128)(2,1)S(1)} async-done(((bf16[64,8,128]{2,1,0:T(8,128)(2,1)}), bf16[64,8,128]{2,1,0:T(8,128)(2,1)S(1)}, u32[]{:S(2)}, u32[]{:S(2)}) %all-to-all-start.1) | async-done | bytes 131104 | tf_op jit(solution)/shard_map/all_to_all | solution.py:101
  82.4 1.2 fusion.67
  83.6 1.2 fusion.66
  84.8 1.2 fusion.69
  86.0 1.2 fusion.68
  87.2 1.2 convolution_add_fusion.5
  88.4 1.2 convolution_subtract_fusion.7
  89.6 1.2 convolution_add_fusion.4
  90.8 1.4 multiply_subtract_fusion.3
  92.3 0.9 fusion.110
  93.1 0.9 fusion.108
  94.0 0.9 convolution_subtract_fusion.6
  94.9 0.9 convolution_add_fusion.3
  95.8 0.8 fusion.23
  96.6 0.8 fusion.5
  98.7 4.6 %all-to-all-start.3 = ((bf16[8,64,128]{2,0,1:T(8,128)(2,1)}), bf16[8,64,128]{2,0,1:T(8,128)(2,1)S(1)}, u32[]{:S(2)}, u32[]{:S(2)}) async-start(bf16[8,64,128]{2,0,1:T(8,128)(2,1)} %fusion.61), calls=%async_computation.3 | async-start | bytes 262144 | tf_op jit(solution)/shard_map/all_to_all | solution.py:111
  103.4 0.8 copy-done.5
  104.3 16.2 %all-to-all-done.3 = bf16[8,64,128]{2,0,1:T(8,128)(2,1)S(1)} async-done(((bf16[8,64,128]{2,0,1:T(8,128)(2,1)}), bf16[8,64,128]{2,0,1:T(8,128)(2,1)S(1)}, u32[]{:S(2)}, u32[]{:S(2)}) %all-to-all-start.3) | async-done | bytes 131104 | tf_op jit(solution)/shard_map/all_to_all | solution.py:111
  120.6 20.4 %all-reduce.3 = (f32[128]{0:T(128)S(1)}, f32[128]{0:T(128)S(1)}) all-reduce(f32[128]{0:T(128)S(1)} %get-tuple-element.16, f32[128]{0:T(128)S(1)} %get-tuple-element.15), channel_id=1, replica_groups=mesh['ctx'=64,'tp'=8] {'tp'}, use_global_device_ids=true, to_apply=%region_1.2 | all-reduce | flops 256 | bytes 2048 | tf_op jit(solution)/shard_map/psum | solution.py:92
  140.9 0.8 fusion.65
  141.8 24.6 %all_to_all.122 = bf16[64,8,128]{2,1,0:T(8,128)(2,1)S(1)} all-to-all(bf16[64,8,128]{2,1,0:T(8,128)(2,1)S(1)} %get-tuple-element.29), channel_id=1, replica_groups=mesh['ctx'=64,'tp'=8] {'ctx'}, dimensions={0} | all-to-all | bytes 262144 | tf_op jit(solution)/shard_map/all_to_all | solution.py:123
  167.7 1.2 fusion.71
  168.9 1.2 fusion.70
  170.1 1.2 convolution_add_fusion.2
  171.3 1.3 multiply_add_fusion
  172.7 0.9 fusion.97
  173.5 0.9 fusion.95
  174.4 0.9 convolution_subtract_fusion.1
  175.3 0.9 convolution_add_fusion
  176.1 0.8 fusion.9
  177.0 0.8 fusion.3
  179.2 4.4 %all-to-all-start.7 = ((bf16[8,64,128]{2,0,1:T(8,128)(2,1)}), bf16[8,64,128]{2,0,1:T(8,128)(2,1)S(1)}, u32[]{:S(2)}, u32[]{:S(2)}) async-start(bf16[8,64,128]{2,0,1:T(8,128)(2,1)} %fusion.62), calls=%async_computation.7 | async-start | bytes 262144 | tf_op jit(solution)/shard_map/all_to_all | solution.py:135
  183.6 0.9 fusion.100
  184.5 0.9 fusion.102
  185.4 0.9 convolution_add_fusion.1
  186.3 0.9 convolution_subtract_fusion.3
  187.1 0.8 fusion.16
  188.0 0.8 fusion.4
  190.1 10.8 %all-to-all-done.7 = bf16[8,64,128]{2,0,1:T(8,128)(2,1)S(1)} async-done(((bf16[8,64,128]{2,0,1:T(8,128)(2,1)}), bf16[8,64,128]{2,0,1:T(8,128)(2,1)S(1)}, u32[]{:S(2)}, u32[]{:S(2)}) %all-to-all-start.7) | async-done | bytes 131104 | tf_op jit(solution)/shard_map/all_to_all | solution.py:135
  200.9 20.8 %all_to_all.123 = bf16[8,64,128]{2,0,1:T(8,128)(2,1)S(1)} all-to-all(bf16[8,64,128]{2,0,1:T(8,128)(2,1)S(1)} %get-tuple-element.27), channel_id=1, replica_groups=mesh['ctx'=64,'tp'=8] {'ctx'}, dimensions={1} | all-to-all | bytes 262144 | tf_op jit(solution)/shard_map/all_to_all | solution.py:134
  221.7 4.6 %all-to-all-start.5 = ((bf16[8,64,128]{2,0,1:T(8,128)(2,1)}), bf16[8,64,128]{2,0,1:T(8,128)(2,1)S(1)}, u32[]{:S(2)}, u32[]{:S(2)}) async-start(bf16[8,64,128]{2,0,1:T(8,128)(2,1)} %get-tuple-element.28), calls=%async_computation.5 | async-start | bytes 262144 | tf_op jit(solution)/shard_map/all_to_all | solution.py:133
  229.5 14.0 %all-to-all-done.5 = bf16[8,64,128]{2,0,1:T(8,128)(2,1)S(1)} async-done(((bf16[8,64,128]{2,0,1:T(8,128)(2,1)}), bf16[8,64,128]{2,0,1:T(8,128)(2,1)S(1)}, u32[]{:S(2)}, u32[]{:S(2)}) %all-to-all-start.5) | async-done | bytes 131104 | tf_op jit(solution)/shard_map/all_to_all | solution.py:133
  (45 shorter events, 14.9 us)
Async XLA Ops:
  2.3 18.2 %copy-start.2 = (bf16[128,512]{1,0:T(8,128)(2,1)S(1)}, bf16[128,512]{1,0:T(8,128)(2,1)}, u32[]{:S(2)}) copy-start(bf16[128,512]{1,0:T(8,128)(2,1)} %param.8) | copy-start | bytes 393220
  2.3 35.3 %all-to-all-start = ((bf16[64,8,128]{2,1,0:T(8,128)(2,1)}), bf16[64,8,128]{2,1,0:T(8,128)(2,1)S(1)}, u32[]{:S(2)}, u32[]{:S(2)}) async-start(bf16[64,8,128]{2,1,0:T(8,128)(2,1)} %bitcast.1), calls=%async_computation | async-start | bytes 262144 | tf_op jit(solution)/shard_map/all_to_all | solution.py:100
  37.6 21.7 %all-to-all-start.2 = ((bf16[64,8,128]{2,1,0:T(8,128)(2,1)}), bf16[64,8,128]{2,1,0:T(8,128)(2,1)S(1)}, u32[]{:S(2)}, u32[]{:S(2)}) async-start(bf16[64,8,128]{2,1,0:T(8,128)(2,1)} %bitcast.13), calls=%async_computation.2 | async-start | bytes 262144 | tf_op jit(solution)/shard_map/all_to_all | solution.py:102
  42.4 0.9 copy-start.3
  59.3 21.7 %all-to-all-start.1 = ((bf16[64,8,128]{2,1,0:T(8,128)(2,1)}), bf16[64,8,128]{2,1,0:T(8,128)(2,1)S(1)}, u32[]{:S(2)}, u32[]{:S(2)}) async-start(bf16[64,8,128]{2,1,0:T(8,128)(2,1)} %bitcast.5), calls=%async_computation.1 | async-start | bytes 262144 | tf_op jit(solution)/shard_map/all_to_all | solution.py:101
  98.6 4.6 %copy-start.4 = (bf16[128,512]{1,0:T(8,128)(2,1)S(1)}, bf16[128,512]{1,0:T(8,128)(2,1)}, u32[]{:S(2)}) copy-start(bf16[128,512]{1,0:T(8,128)(2,1)} %param.5) | copy-start | bytes 393220
  98.7 21.8 %all-to-all-start.3 = ((bf16[8,64,128]{2,0,1:T(8,128)(2,1)}), bf16[8,64,128]{2,0,1:T(8,128)(2,1)S(1)}, u32[]{:S(2)}, u32[]{:S(2)}) async-start(bf16[8,64,128]{2,0,1:T(8,128)(2,1)} %fusion.61), calls=%async_computation.3 | async-start | bytes 262144 | tf_op jit(solution)/shard_map/all_to_all | solution.py:111
  103.3 0.9 copy-start.5
  179.2 21.7 %all-to-all-start.7 = ((bf16[8,64,128]{2,0,1:T(8,128)(2,1)}), bf16[8,64,128]{2,0,1:T(8,128)(2,1)S(1)}, u32[]{:S(2)}, u32[]{:S(2)}) async-start(bf16[8,64,128]{2,0,1:T(8,128)(2,1)} %fusion.62), calls=%async_computation.7 | async-start | bytes 262144 | tf_op jit(solution)/shard_map/all_to_all | solution.py:135
  221.7 4.6 %copy-start.1 = (bf16[128,512]{0,1:T(8,128)(2,1)S(1)}, bf16[128,512]{0,1:T(8,128)(2,1)}, u32[]{:S(2)}) copy-start(bf16[128,512]{0,1:T(8,128)(2,1)} %get-tuple-element.30) | copy-start | bytes 393220
  221.7 21.8 %all-to-all-start.5 = ((bf16[8,64,128]{2,0,1:T(8,128)(2,1)}), bf16[8,64,128]{2,0,1:T(8,128)(2,1)S(1)}, u32[]{:S(2)}, u32[]{:S(2)}) async-start(bf16[8,64,128]{2,0,1:T(8,128)(2,1)} %get-tuple-element.28), calls=%async_computation.5 | async-start | bytes 262144 | tf_op jit(solution)/shard_map/all_to_all | solution.py:133
  226.3 0.9 copy-start
where the time goes:
time: 248 us; the launch traced here: 245 us
  waiting for transfers between devices  88.3 us (36%)
  blocking collectives  65.8 us (27%)
  starting transfers between devices  40.9 us (16%)
  matrix products  34 us (14%)
  local copies, waits for them, and re-layouts  10.6 us (4%)
  other arithmetic  3.55 us (1%)
    dot_general x24, matrix products, right_apply(): return jnp.einsum('cka,ab->ckb', blocks, table, precision=precise)  25.1 us
    all_to_all x1, blocking collectives, per_device(): lax.all_to_all(gconv.T, 'ctx', split_axis=0, concat_axis=1, tiled=True)  24.6 us
    all_to_all x1, blocking collectives, per_device(): lax.all_to_all(dvalue_cols, 'ctx', split_axis=1, concat_axis=0, tiled=True)  20.8 us
    psum x1, blocking collectives, channel_total(): return lax.psum(values, 'tp')  20.4 us
    all_to_all x1, starting transfers between devices, per_device(): lax.all_to_all(key_proj.T, 'ctx', split_axis=0, concat_axis=1, tiled=True)  18.2 us
    all_to_all x1, waiting for transfers between devices, per_device(): lax.all_to_all(key_proj.T, 'ctx', split_axis=0, concat_axis=1, tiled=True)  16.4 us
    all_to_all x1, waiting for transfers between devices, per_device(): lax.all_to_all(conv_cols, 'ctx', split_axis=1, concat_axis=0, tiled=True)  16.2 us
    all_to_all x1, waiting for transfers between devices, per_device(): lax.all_to_all(value_proj.T, 'ctx', split_axis=0, concat_axis=1, tiled=True)  15.7 us
  transfers between devices with their start and end apart: 6, of which 6 were waited for; matrix products, arithmetic and copies ran while one was open for 5% of the time, Pallas kernels for 0%

commit v1 on v0

--- a/solution.py
+++ b/solution.py
@@ -89,7 +89,7 @@
 
 
 def channel_total(values):
-    return lax.psum(values, "tp")
+    return jnp.sum(lax.all_gather(values, "tp"), axis=0)
 
 
 def per_device(query, key_proj, value_proj, filter_taps, grad_out):

time: 248 us -> 265 us (1.069)
  blocking collectives: 65.8 us -> 82.8 us
    all_gather x0 -> x2, blocking collectives: none -> 33.9 us  [channel_total(): return jnp.sum(lax.all_gather(values, 'tp'), axis=0)]
    psum x1 -> x0, blocking collectives: 20.4 us -> none  [channel_total(): return lax.psum(values, 'tp')]
    all_to_all x1, blocking collectives: 24.6 us -> 28.1 us  [per_device(): lax.all_to_all(gconv.T, 'ctx', split_axis=0, concat_axis=1, tiled=True)]
where the time goes in v1:
time: 265 us; the launch traced here: 262 us
  waiting for transfers between devices  88.3 us (33%)
  blocking collectives  82.8 us (31%)
  starting transfers between devices  40.9 us (15%)
  matrix products  34 us (13%)
  local copies, waits for them, and re-layouts  10.6 us (4%)
  other arithmetic  3.6 us (1%)
    all_gather x2, blocking collectives, channel_total(): return jnp.sum(lax.all_gather(values, 'tp'), axis=0)  33.9 us
    all_to_all x1, blocking collectives, per_device(): lax.all_to_all(gconv.T, 'ctx', split_axis=0, concat_axis=1, tiled=True)  28.1 us
    dot_general x24, matrix products, right_apply(): return jnp.einsum('cka,ab->ckb', blocks, table, precision=precise)  25.1 us
    all_to_all x1, blocking collectives, per_device(): lax.all_to_all(dvalue_cols, 'ctx', split_axis=1, concat_axis=0, tiled=True)  20.8 us
    all_to_all x1, starting transfers between devices, per_device(): lax.all_to_all(key_proj.T, 'ctx', split_axis=0, concat_axis=1, tiled=True)  18.2 us
    all_to_all x1, waiting for transfers between devices, per_device(): lax.all_to_all(key_proj.T, 'ctx', split_axis=0, concat_axis=1, tiled=True)  16.4 us
    all_to_all x1, waiting for transfers between devices, per_device(): lax.all_to_all(conv_cols, 'ctx', split_axis=1, concat_axis=0, tiled=True)  16.2 us
    all_to_all x1, waiting for transfers between devices, per_device(): lax.all_to_all(value_proj.T, 'ctx', split_axis=0, concat_axis=1, tiled=True)  15.7 us
  transfers between devices with their start and end apart: 6, of which 6 were waited for; matrix products, arithmetic and copies ran while one was open for 5% of the time, Pallas kernels for 0%

profile of v1, /device:TPU:1, one launch (start us, length us, event | category | flops | bytes accessed | tf_op | source)
XLA Modules:
  0.0 261.6 jit_solution(17741919336070045547)
XLA Ops:
  0.6 1.7 copy.86
  2.3 18.2 %all-to-all-start = ((bf16[64,8,128]{2,1,0:T(8,128)(2,1)}), bf16[64,8,128]{2,1,0:T(8,128)(2,1)S(1)}, u32[]{:S(2)}, u32[]{:S(2)}) async-start(bf16[64,8,128]{2,1,0:T(8,128)(2,1)} %bitcast.1), calls=%async_computation | async-start | bytes 262144 | tf_op jit(solution)/shard_map/all_to_all | solution.py:100
  21.3 16.4 %all-to-all-done = bf16[64,8,128]{2,1,0:T(8,128)(2,1)S(1)} async-done(((bf16[64,8,128]{2,1,0:T(8,128)(2,1)}), bf16[64,8,128]{2,1,0:T(8,128)(2,1)S(1)}, u32[]{:S(2)}, u32[]{:S(2)}) %all-to-all-start) | async-done | bytes 131104 | tf_op jit(solution)/shard_map/all_to_all | solution.py:100
  37.6 4.4 %all-to-all-start.2 = ((bf16[64,8,128]{2,1,0:T(8,128)(2,1)}), bf16[64,8,128]{2,1,0:T(8,128)(2,1)S(1)}, u32[]{:S(2)}, u32[]{:S(2)}) async-start(bf16[64,8,128]{2,1,0:T(8,128)(2,1)} %bitcast.13), calls=%async_computation.2 | async-start | bytes 262144 | tf_op jit(solution)/shard_map/all_to_all | solution.py:102
  44.1 15.2 %all-to-all-done.2 = bf16[64,8,128]{2,1,0:T(8,128)(2,1)S(1)} async-done(((bf16[64,8,128]{2,1,0:T(8,128)(2,1)}), bf16[64,8,128]{2,1,0:T(8,128)(2,1)S(1)}, u32[]{:S(2)}, u32[]{:S(2)}) %all-to-all-start.2) | async-done | bytes 131104 | tf_op jit(solution)/shard_map/all_to_all | solution.py:102
  59.3 4.6 %all-to-all-start.1 = ((bf16[64,8,128]{2,1,0:T(8,128)(2,1)}), bf16[64,8,128]{2,1,0:T(8,128)(2,1)S(1)}, u32[]{:S(2)}, u32[]{:S(2)}) async-start(bf16[64,8,128]{2,1,0:T(8,128)(2,1)} %bitcast.5), calls=%async_computation.1 | async-start | bytes 262144 | tf_op jit(solution)/shard_map/all_to_all | solution.py:101
  65.3 15.7 %all-to-all-done.1 = bf16[64,8,128]{2,1,0:T(8,128)(2,1)S(1)} async-done(((bf16[64,8,128]{2,1,0:T(8,128)(2,1)}), bf16[64,8,128]{2,1,0:T(8,128)(2,1)S(1)}, u32[]{:S(2)}, u32[]{:S(2)}) %all-to-all-start.1) | async-done | bytes 131104 | tf_op jit(solution)/shard_map/all_to_all | solution.py:101
  82.4 1.2 fusion.67
  83.6 1.2 fusion.66
  84.8 1.2 fusion.69
  86.0 1.2 fusion.68
  87.2 1.2 convolution_add_fusion.5
  88.4 1.2 convolution_subtract_fusion.7
  89.6 1.2 convolution_add_fusion.4
  90.8 1.4 multiply_subtract_fusion.3
  92.3 0.9 fusion.110
  93.1 0.9 fusion.108
  94.0 0.9 convolution_subtract_fusion.6
  94.9 0.9 convolution_add_fusion.3
  95.8 0.8 fusion.23
  96.6 0.8 fusion.5
  98.7 4.6 %all-to-all-start.3 = ((bf16[8,64,128]{2,0,1:T(8,128)(2,1)}), bf16[8,64,128]{2,0,1:T(8,128)(2,1)S(1)}, u32[]{:S(2)}, u32[]{:S(2)}) async-start(bf16[8,64,128]{2,0,1:T(8,128)(2,1)} %fusion.61), calls=%async_computation.3 | async-start | bytes 262144 | tf_op jit(solution)/shard_map/all_to_all | solution.py:111
  104.3 16.2 %all-to-all-done.3 = bf16[8,64,128]{2,0,1:T(8,128)(2,1)S(1)} async-done(((bf16[8,64,128]{2,0,1:T(8,128)(2,1)}), bf16[8,64,128]{2,0,1:T(8,128)(2,1)S(1)}, u32[]{:S(2)}, u32[]{:S(2)}) %all-to-all-start.3) | async-done | bytes 131104 | tf_op jit(solution)/shard_map/all_to_all | solution.py:111
  120.6 19.4 %all-gather.2 = f32[8,1,128]{2,1,0:T(1,128)S(1)} all-gather(f32[1,1,128]{2,1,0:T(1,128)S(1)} %bitcast.236), channel_id=2, replica_groups=mesh['ctx'=64,'tp'=8] {'tp'}, dimensions={0}, use_global_device_ids=true | all-gather | bytes 4608 | tf_op jit(solution)/shard_map/all_gather | solution.py:92
  140.0 14.5 %all-gather.3 = f32[8,1,128]{2,1,0:T(1,128)S(1)} all-gather(f32[1,1,128]{2,1,0:T(1,128)S(1)} %bitcast.235), channel_id=3, replica_groups=mesh['ctx'=64,'tp'=8] {'tp'}, dimensions={0}, use_global_device_ids=true | all-gather | bytes 4608 | tf_op jit(solution)/shard_map/all_gather | solution.py:92
  154.5 0.8 fusion.65
  155.3 28.1 %all_to_all.122 = bf16[64,8,128]{2,1,0:T(8,128)(2,1)S(1)} all-to-all(bf16[64,8,128]{2,1,0:T(8,128)(2,1)S(1)} %get-tuple-element.27), channel_id=1, replica_groups=mesh['ctx'=64,'tp'=8] {'ctx'}, dimensions={0} | all-to-all | bytes 262144 | tf_op jit(solution)/shard_map/all_to_all | solution.py:123
  184.8 1.2 fusion.71
  186.0 1.2 fusion.70
  187.2 1.2 convolution_add_fusion.2
  188.4 1.3 multiply_add_fusion
  189.7 0.9 fusion.97
  190.6 0.9 fusion.95
  191.5 0.9 convolution_subtract_fusion.1
  192.3 0.9 convolution_add_fusion
  193.2 0.8 fusion.9
  194.0 0.8 fusion.3
  196.3 4.5 %all-to-all-start.7 = ((bf16[8,64,128]{2,0,1:T(8,128)(2,1)}), bf16[8,64,128]{2,0,1:T(8,128)(2,1)S(1)}, u32[]{:S(2)}, u32[]{:S(2)}) async-start(bf16[8,64,128]{2,0,1:T(8,128)(2,1)} %fusion.62), calls=%async_computation.7 | async-start | bytes 262144 | tf_op jit(solution)/shard_map/all_to_all | solution.py:135
  200.7 0.9 fusion.100
  201.6 0.9 fusion.102
  202.5 0.9 convolution_add_fusion.1
  203.3 0.9 convolution_subtract_fusion.3
  204.2 0.8 fusion.16
  205.0 0.8 fusion.4
  207.1 10.8 %all-to-all-done.7 = bf16[8,64,128]{2,0,1:T(8,128)(2,1)S(1)} async-done(((bf16[8,64,128]{2,0,1:T(8,128)(2,1)}), bf16[8,64,128]{2,0,1:T(8,128)(2,1)S(1)}, u32[]{:S(2)}, u32[]{:S(2)}) %all-to-all-start.7) | async-done | bytes 131104 | tf_op jit(solution)/shard_map/all_to_all | solution.py:135
  217.9 20.8 %all_to_all.123 = bf16[8,64,128]{2,0,1:T(8,128)(2,1)S(1)} all-to-all(bf16[8,64,128]{2,0,1:T(8,128)(2,1)S(1)} %get-tuple-element.25), channel_id=1, replica_groups=mesh['ctx'=64,'tp'=8] {'ctx'}, dimensions={1} | all-to-all | bytes 262144 | tf_op jit(solution)/shard_map/all_to_all | solution.py:134
  238.8 4.6 %all-to-all-start.5 = ((bf16[8,64,128]{2,0,1:T(8,128)(2,1)}), bf16[8,64,128]{2,0,1:T(8,128)(2,1)S(1)}, u32[]{:S(2)}, u32[]{:S(2)}) async-start(bf16[8,64,128]{2,0,1:T(8,128)(2,1)} %get-tuple-element.26), calls=%async_computation.5 | async-start | bytes 262144 | tf_op jit(solution)/shard_map/all_to_all | solution.py:133
  246.6 14.0 %all-to-all-done.5 = bf16[8,64,128]{2,0,1:T(8,128)(2,1)S(1)} async-done(((bf16[8,64,128]{2,0,1:T(8,128)(2,1)}), bf16[8,64,128]{2,0,1:T(8,128)(2,1)S(1)}, u32[]{:S(2)}, u32[]{:S(2)}) %all-to-all-start.5) | async-done | bytes 131104 | tf_op jit(solution)/shard_map/all_to_all | solution.py:133
  (48 shorter events, 15.7 us)
Async XLA Ops:
  2.3 18.2 %copy-start.2 = (bf16[128,512]{1,0:T(8,128)(2,1)S(1)}, bf16[128,512]{1,0:T(8,128)(2,1)}, u32[]{:S(2)}) copy-start(bf16[128,512]{1,0:T(8,128)(2,1)} %param.8) | copy-start | bytes 393220
  2.3 35.3 %all-to-all-start = ((bf16[64,8,128]{2,1,0:T(8,128)(2,1)}), bf16[64,8,128]{2,1,0:T(8,128)(2,1)S(1)}, u32[]{:S(2)}, u32[]{:S(2)}) async-start(bf16[64,8,128]{2,1,0:T(8,128)(2,1)} %bitcast.1), calls=%async_computation | async-start | bytes 262144 | tf_op jit(solution)/shard_map/all_to_all | solution.py:100
  37.6 21.7 %all-to-all-start.2 = ((bf16[64,8,128]{2,1,0:T(8,128)(2,1)}), bf16[64,8,128]{2,1,0:T(8,128)(2,1)S(1)}, u32[]{:S(2)}, u32[]{:S(2)}) async-start(bf16[64,8,128]{2,1,0:T(8,128)(2,1)} %bitcast.13), calls=%async_computation.2 | async-start | bytes 262144 | tf_op jit(solution)/shard_map/all_to_all | solution.py:102
  42.4 0.9 copy-start.3
  59.3 21.7 %all-to-all-start.1 = ((bf16[64,8,128]{2,1,0:T(8,128)(2,1)}), bf16[64,8,128]{2,1,0:T(8,128)(2,1)S(1)}, u32[]{:S(2)}, u32[]{:S(2)}) async-start(bf16[64,8,128]{2,1,0:T(8,128)(2,1)} %bitcast.5), calls=%async_computation.1 | async-start | bytes 262144 | tf_op jit(solution)/shard_map/all_to_all | solution.py:101
  98.6 4.6 %copy-start.4 = (bf16[128,512]{1,0:T(8,128)(2,1)S(1)}, bf16[128,512]{1,0:T(8,128)(2,1)}, u32[]{:S(2)}) copy-start(bf16[128,512]{1,0:T(8,128)(2,1)} %param.5) | copy-start | bytes 393220
  98.7 21.8 %all-to-all-start.3 = ((bf16[8,64,128]{2,0,1:T(8,128)(2,1)}), bf16[8,64,128]{2,0,1:T(8,128)(2,1)S(1)}, u32[]{:S(2)}, u32[]{:S(2)}) async-start(bf16[8,64,128]{2,0,1:T(8,128)(2,1)} %fusion.61), calls=%async_computation.3 | async-start | bytes 262144 | tf_op jit(solution)/shard_map/all_to_all | solution.py:111
  103.3 0.9 copy-start.5
  196.3 21.7 %all-to-all-start.7 = ((bf16[8,64,128]{2,0,1:T(8,128)(2,1)}), bf16[8,64,128]{2,0,1:T(8,128)(2,1)S(1)}, u32[]{:S(2)}, u32[]{:S(2)}) async-start(bf16[8,64,128]{2,0,1:T(8,128)(2,1)} %fusion.62), calls=%async_computation.7 | async-start | bytes 262144 | tf_op jit(solution)/shard_map/all_to_all | solution.py:135
  238.8 4.6 %copy-start.1 = (bf16[128,512]{0,1:T(8,128)(2,1)S(1)}, bf16[128,512]{0,1:T(8,128)(2,1)}, u32[]{:S(2)}) copy-start(bf16[128,512]{0,1:T(8,128)(2,1)} %get-tuple-element.28) | copy-start | bytes 393220
  238.8 21.8 %all-to-all-start.5 = ((bf16[8,64,128]{2,0,1:T(8,128)(2,1)}), bf16[8,64,128]{2,0,1:T(8,128)(2,1)S(1)}, u32[]{:S(2)}, u32[]{:S(2)}) async-start(bf16[8,64,128]{2,0,1:T(8,128)(2,1)} %get-tuple-element.26), calls=%async_computation.5 | async-start | bytes 262144 | tf_op jit(solution)/shard_map/all_to_all | solution.py:133
  243.4 0.9 copy-start
